TPU v7x, 32 devices: a whole 2x2x4 slice. The times are simulated.
32 devices in a mesh: groups: 2 (over x), tensor: 16 (over z, y, core).
Axes of the slice: x: 2, y: 2, z: 4, core: 2. Of those that a mesh axis runs over, the one named last changes fastest.
Arguments:
- tokens: bfloat16 [256, 8192], P(('groups', 'tensor')), parts along dimension 0, may hold values from -6 to 6
- adapter_ids: int32 [256], P(('groups', 'tensor')), parts along dimension 0, may hold values from 0 to 15, as said below
- gate_weight: bfloat16 [8192, 16384], P(None, 'tensor'), may hold values from -0.0625 to 0.0625
- up_weight: bfloat16 [8192, 16384], P(None, 'tensor'), may hold values from -0.0625 to 0.0625
- shrink_factors: bfloat16 [16, 8192, 64], P('tensor'), may hold values from -0.0625 to 0.0625
- expand_factors: bfloat16 [16, 64, 16384], P(None, None, 'tensor'), may hold values from -0.75 to 0.75
Outputs:
- hidden: bfloat16 [256, 16384], P('groups', 'tensor'), parts along dimension 0
There are 2 independent parts, one for each index of `groups`. A program takes and returns all parts, laid end to end along the dimension named above; an argument that names none is the same for every part. Nothing has to cross between parts.
Inputs may be any that keep to these rules, and one draw needn't show every extreme that they name: `adapter_ids`: no adapter is named by more than 32 rows of a group, and one adapter by exactly 32.
All inputs are finite; a program needn't handle non-finite values.
Results may differ from a plain program's by a relative error of at most 0.0037.
Values may be sent and summed in bfloat16 or wider, within the bound.
A program may use at most 128 MiB of HBM per device.

v0:
```python
import jax
import jax.numpy as jnp
from jax import lax
from jax.sharding import PartitionSpec as P


def absorb_rows(gate_weight, up_weight, piece_rows):
    gate_part = jnp.dot(piece_rows, gate_weight, preferred_element_type=jnp.float32)
    up_part = jnp.dot(piece_rows, up_weight, preferred_element_type=jnp.float32)
    return (gate_part, up_part, piece_rows)


def local(tokens, adapter_ids, gate_weight, up_weight, shrink_factors, expand_factors):
    devices = lax.axis_size("tensor")
    row_count = tokens.shape[0] * devices
    hidden_width = gate_weight.shape[1]
    rank_width = shrink_factors.shape[2]
    adapter_count = expand_factors.shape[0]
    gate_sum, up_sum, rows_all = absorb_rows(
        gate_weight, up_weight, lax.all_gather(tokens, "tensor", axis=0, tiled=True)
    )
    ids_all = lax.all_gather(adapter_ids, "tensor", axis=0, tiled=True)
    one_hot = ids_all[:, None] == jnp.arange(adapter_count, dtype=jnp.int32)[None, :]
    owned = lax.axis_index("tensor")
    capacity = 4 * tokens.shape[0]
    is_mine = ids_all == owned
    order_keys = jnp.where(is_mine, 0, row_count) + jnp.arange(row_count, dtype=jnp.int32)
    chosen = jnp.argsort(order_keys)[:capacity]
    is_valid = jnp.take(is_mine, chosen).astype(jnp.float32)
    chosen_rows = jnp.take(rows_all, chosen, axis=0)
    product = (
        jnp.dot(chosen_rows, shrink_factors[0], preferred_element_type=jnp.float32)
        * is_valid[:, None]
    )
    partial_sum = jnp.zeros((row_count, rank_width), jnp.float32).at[chosen].add(product)
    shrunk = lax.psum(partial_sum, "tensor").astype(jnp.bfloat16)
    wide_rows = jnp.where(
        one_hot[:, :, None], shrunk[:, None, :], jnp.zeros((), jnp.bfloat16)
    ).reshape(row_count, adapter_count * rank_width)
    delta_up = jnp.dot(
        wide_rows,
        expand_factors.reshape(adapter_count * rank_width, hidden_width),
        preferred_element_type=jnp.float32,
    )
    return (jax.nn.silu(gate_sum) * (up_sum + delta_up)).astype(jnp.bfloat16)


def solution(mesh):
    return jax.shard_map(
        local,
        mesh=mesh,
        in_specs=(
            P(("groups", "tensor"), None),
            P(("groups", "tensor")),
            P(None, "tensor"),
            P(None, "tensor"),
            P("tensor", None, None),
            P(None, None, "tensor"),
        ),
        out_specs=P("groups", "tensor"),
        check_vma=False,
    )
```

profile of v0, /device:TPU:0, one launch (start us, length us, event | category | flops | bytes accessed | tf_op | source)
XLA Modules:
  0.0 141.5 jit_solution(17458966511923156825)
XLA Ops:
  6.5 0.0 copy-start
  6.5 0.0 all-gather.2.cloned.1.call-start
  6.5 0.7 all-gather.2.cloned.1.call-update
  7.3 1.2 dynamic-slice
  9.2 0.9 dynamic-update-slice
  10.0 13.7 %all-reduce = s32[128]{0:T(128)S(1)} all-reduce(s32[128]{0:T(128)S(1)} %dynamic-update-slice), channel_id=1, replica_groups=mesh['groups'=2,'tensor'=16] {'tensor'}, use_global_device_ids=true, to_apply=%add | all-reduce | flops 128 | bytes 1024
  23.8 2.5 %sort.17 = (s32[128]{0:T(128)}, s32[128]{0:T(128)S(1)}) sort(s32[128]{0:T(128)S(1)} %get-tuple-element.9, s32[128]{0:T(128)S(1)} %iota.15), dimensions={0}, to_apply=%region_0.1 | sort | flops 896 | bytes 2048 | tf_op jit(solution)/shard_map/jit(argsort)/sort | solution.py:28
  26.3 0.7 gather_fusion.1
  27.0 27.0 %all-gather.2.cloned.1.call-done = bf16[128,8192]{1,0:T(8,128)(2,1)} async-done(((bf16[8,8192]{1,0:T(8,128)(2,1)}), bf16[128,8192]{1,0:T(8,128)(2,1)}) %all-gather.2.cloned.1.call-update) | async-done | bytes 2097168 | tf_op jit(solution)/shard_map/all_gather | solution.py:20
  54.1 3.2 %gather_fusion = bf16[32,8192]{1,0:T(8,128)(2,1)S(1)} fusion(bf16[128,8192]{1,0:T(8,128)(2,1)} %all-gather.2.cloned.1.call-done, s32[1024]{0:T(1024)S(1)} %pad_clamp_fusion), kind=kCustom, calls=%fused_computation | custom fusion | bytes 1048704 | tf_op jit(solution)/shard_map/jit(_take)/gather | solution.py:30
  57.3 1.7 %convolution_multiply_fusion = f32[32,64]{1,0:T(8,128)S(1)} fusion(bf16[1,8192,64]{1,2,0:T(8,128)(2,1)} %param.10, bf16[32,8192]{1,0:T(8,128)(2,1)S(1)} %gather_fusion, pred[32]{0:T(512)(128)(4,1)S(1)} %get-tuple-element.7, f32[32]{0:T(128)S(1)} %select_convert_fusion), kind=kOutput, calls=%fused_computation.7 | convolution fusion | flops 33818624 | bytes 1581216 | tf_op jit(solution)/shard_map/dot_general | solution.py:32
  59.0 0.7 scatter_custom_fusion
  59.7 0.1 copy.8
  59.8 59.5 %psum.7 = bf16[128,64]{0,1:T(8,128)(2,1)S(1)} all-reduce(f32[128,64]{0,1:T(8,128)S(1)} %copy.8), channel_id=1, replica_groups=mesh['groups'=2,'tensor'=16] {'tensor'}, use_global_device_ids=true, to_apply=%region_2.3 | all-reduce | flops 8192 | bytes 49152 | tf_op jit(solution)/shard_map/psum | solution.py:36
  119.2 0.0 copy-done
  119.3 0.0 copy-start.1
  119.3 0.5 convolution_bitcast_fusion
  119.7 1.1 copy-done.1
  120.8 0.0 copy-start.2
  120.8 8.4 %fusion.14 = f32[128,1024]{1,0:T(8,128)S(1)} fusion(bf16[128,8192]{1,0:T(8,128)(2,1)S(1)} %copy-done.1, bf16[8192,1024]{1,0:T(8,128)(2,1)} %param.8), kind=kOutput, calls=%fused_computation.27 | convolution fusion | flops 2147483648 | bytes 19398656 | tf_op jit(solution)/shard_map/dot_general | solution.py:8
  129.3 2.1 %copy-done.2 = bf16[8192,1024]{1,0:T(8,128)(2,1)S(1)} copy-done((bf16[8192,1024]{1,0:T(8,128)(2,1)S(1)}, bf16[8192,1024]{1,0:T(8,128)(2,1)}, u32[]{:S(2)}) %copy-start.2) | copy-done | bytes 16777240
  131.4 3.2 %fusion.1 = bf16[128,1024]{1,0:T(8,128)(2,1)} fusion(f32[128,1024]{1,0:T(8,128)S(1)} %convolution_bitcast_fusion, bf16[128,8192]{1,0:T(8,128)(2,1)S(1)} %copy-done.1, bf16[8192,1024]{1,0:T(8,128)(2,1)S(1)} %copy-done.2, f32[128,1024]{1,0:T(8,128)S(1)} %fusion.14), kind=kOutput, calls=%fused_computation.6 | convolution fusion | flops 2148401152 | bytes 20185088 | tf_op jit(solution)/shard_map/dot_general | solution.py:9
  (7 shorter events, 0.0 us)
Async XLA Ops:
  6.5 112.7 %copy-start = (bf16[16,64,1024]{2,1,0:T(8,128)(2,1)S(1)}, bf16[16,64,1024]{2,1,0:T(8,128)(2,1)}, u32[]{:S(2)}) copy-start(bf16[16,64,1024]{2,1,0:T(8,128)(2,1)} %param.11) | copy-start | bytes 6291460
  6.5 47.5 %all-gather.2.cloned.1.call-start = ((), (), s32[]{:S(2)}) async-start(), calls=%async_computation | async-start | bytes 2228224 | tf_op jit(solution)/shard_map/all_gather | solution.py:20
  119.3 1.6 %copy-start.1 = (bf16[128,8192]{1,0:T(8,128)(2,1)S(1)}, bf16[128,8192]{1,0:T(8,128)(2,1)}, u32[]{:S(2)}) copy-start(bf16[128,8192]{1,0:T(8,128)(2,1)} %all-gather.2.cloned.1.call-done) | copy-start | bytes 6291460
  120.8 10.5 %copy-start.2 = (bf16[8192,1024]{1,0:T(8,128)(2,1)S(1)}, bf16[8192,1024]{1,0:T(8,128)(2,1)}, u32[]{:S(2)}) copy-start(bf16[8192,1024]{1,0:T(8,128)(2,1)} %param.9) | copy-start | bytes 50331652
Sparse Core Ops, SparseCore 0:
  9.5 44.4 all-gather.1
where the time goes:
time: 142 us; the launch traced here: 141 us
  blocking collectives  73.2 us (52%)
  waiting for transfers between devices  27.7 us (20%)
  between operations  14.1 us (10%)
  matrix products  13.8 us (10%)
  local copies, waits for them, and re-layouts  9.32 us (7%)
  other arithmetic  3.31 us (2%)
    psum x1, blocking collectives, local(): shrunk = lax.psum(partial_sum, 'tensor').astype(jnp.bfloat16)  59.5 us
    all_gather x1, waiting for transfers between devices, local(): lax.all_gather(tokens, 'tensor', axis=0, tiled=True)  27 us
    unnamed x1, blocking collectives  13.7 us
    dot_general x1, matrix products, absorb_rows(): jnp.dot(piece_rows, gate_weight, preferred_element_type=jnp.float32)  8.41 us
    unnamed x9, local copies, waits for them, and re-layouts  5.35 us
    dot_general x1, matrix products, absorb_rows(): up_part = jnp.dot(piece_rows, up_weight, preferred_element_type=jnp.float32)  3.23 us
    gather x1, local copies, waits for them, and re-layouts, local(): chosen_rows = jnp.take(rows_all, chosen, axis=0)  3.2 us
  transfers between devices with their start and end apart: 1, of which 1 were waited for; matrix products, arithmetic and copies ran while one was open for 4% of the time, Pallas kernels for 0%

commit v1 on v0

v1 whole, which is shorter than its diff:
```python
import functools

import jax
import jax.numpy as jnp
from jax import lax
from jax.experimental import pallas as pl
from jax.experimental.pallas import tpu as pltpu
from jax.sharding import PartitionSpec as P

CORES = 2
LAG = 2


def each(count, body):
    if count <= 4:
        for i in range(count):
            body(i)
    else:
        lax.fori_loop(0, count, lambda i, carry: (body(i), carry)[1], 0)


def step_kernel(
    line, pairs, pieces,
    tokens, ids, gate_weight, up_weight, shrink, expand,
    out,
    rows_in, gate_in, up_in, shrink_in, expand_in, left, gate_acc, up_acc, shrink_acc,
    id_rows, packed, slots_of, wide,
    own_sem, gate_sem, up_sem, small_sem, z_send, z_recv, y_send, y_recv, c_send, c_recv,
    id_send, id_recv, p_send, p_recv,
):
    total = line * pairs * CORES
    row_dev = tokens.shape[0]
    rows = total * row_dev
    depth = tokens.shape[1] // pieces
    rank = shrink.shape[1]
    half = packed.shape[1]
    adapters = expand.shape[0] // rank

    me = lax.axis_index("tensor")
    k = lax.rem(me, CORES)
    y = lax.rem(me // CORES, pairs)
    z = me // (CORES * pairs)

    def place(zz, yy, kk):
        return {"tensor": (zz * pairs + yy) * CORES + kk}

    def peer(i):
        return {"tensor": lax.rem(me + 1 + i, total)}

    def own_copy(c):
        return pltpu.make_async_copy(
            tokens.at[:, pl.ds(c * depth, depth)], rows_in.at[c, k, y, z], own_sem.at[c]
        )

    def gate_copy(c):
        where = pl.ds(pl.multiple_of(c * depth, depth), depth)
        return pltpu.make_async_copy(gate_weight.at[where], gate_in.at[where], gate_sem.at[c])

    def up_copy(c):
        where = pl.ds(pl.multiple_of(c * depth, depth), depth)
        return pltpu.make_async_copy(up_weight.at[where], up_in.at[where], up_sem.at[c])

    shrink_copy = pltpu.make_async_copy(shrink, shrink_in, small_sem.at[0])
    expand_copy = pltpu.make_async_copy(expand, expand_in, small_sem.at[1])

    def z_copy(c, d):
        block = rows_in.at[c, k, y, z]
        return pltpu.make_async_remote_copy(
            block, block, z_send.at[c, d], z_recv.at[c, d],
            device_id=place(lax.rem(z + d + 1, line), y, k), device_id_type=pl.DeviceIdType.MESH,
        )

    def y_copy(c):
        block = rows_in.at[c, k, y]
        return pltpu.make_async_remote_copy(
            block, block, y_send.at[c], y_recv.at[c],
            device_id=place(z, 1 - y, k), device_id_type=pl.DeviceIdType.MESH,
        )

    def c_copy(c):
        block = rows_in.at[c, k]
        return pltpu.make_async_remote_copy(
            block, block, c_send.at[c], c_recv.at[c],
            device_id=place(z, y, 1 - k), device_id_type=pl.DeviceIdType.MESH,
        )

    def id_copy(i):
        return pltpu.make_async_remote_copy(
            id_rows.at[me], id_rows.at[me], id_send, id_recv,
            device_id=peer(i), device_id_type=pl.DeviceIdType.MESH,
        )

    def p_copy(i):
        return pltpu.make_async_remote_copy(
            packed.at[me], packed.at[me], p_send, p_recv,
            device_id=peer(i), device_id_type=pl.DeviceIdType.MESH,
        )

    def wait_all(ref, sem):
        part = ref.at[pl.ds(0, total - 1)]
        pltpu.make_async_copy(part, part, sem).wait()

    barrier = pltpu.get_barrier_semaphore()
    each(total - 1, lambda i: pl.semaphore_signal(
        barrier, inc=1, device_id=peer(i), device_id_type=pl.DeviceIdType.MESH))

    for c in range(pieces):
        own_copy(c).start()
    shrink_copy.start()
    for c in range(pieces):
        gate_copy(c).start()
        up_copy(c).start()
    expand_copy.start()

    lane = lax.broadcasted_iota(jnp.int32, (1, rows), 1)
    id_row = jnp.zeros((1, rows), jnp.int32)
    for j in range(row_dev):
        id_row = jnp.where(lax.rem(lane, row_dev) == j, ids[j], id_row)
    id_rows[me] = id_row
    gate_acc[...] = jnp.zeros_like(gate_acc)
    up_acc[...] = jnp.zeros_like(up_acc)
    shrink_acc[...] = jnp.zeros_like(shrink_acc)
    for c in range(pieces):
        own_copy(c).wait()

    pl.semaphore_wait(barrier, total - 1)
    for c in range(pieces):
        each(line - 1, lambda d, c=c: z_copy(c, d).start())
        if c == 0:
            each(total - 1, lambda i: id_copy(i).start())

    wait_all(id_rows, id_recv)
    owner = lax.broadcasted_iota(jnp.int32, (total, 1, rows), 0)
    lane3 = lax.broadcasted_iota(jnp.int32, (total, 1, rows), 2)
    id_row = jnp.sum(jnp.where(lane3 // row_dev == owner, id_rows[...], 0), axis=0)
    across = lax.broadcasted_iota(jnp.int32, (rows, rows), 1)
    down = lax.broadcasted_iota(jnp.int32, (rows, rows), 0)
    id_wide = jnp.broadcast_to(id_row, (rows, rows)).astype(jnp.float32)
    id_col = jnp.sum(jnp.where(across == down, id_wide, 0.0), axis=1, keepdims=True)
    same = jnp.where(id_wide == id_col, 1.0, 0.0)
    slot_col = jnp.sum(jnp.where(across < down, same, 0.0), axis=1, keepdims=True)
    slot_row = jnp.sum(jnp.where(down < across, same, 0.0), axis=0, keepdims=True)
    slots_of[0] = jnp.broadcast_to(id_col, (rows, 128))
    slots_of[1] = jnp.broadcast_to(slot_col, (rows, 128))
    mine = id_row.astype(jnp.float32) == me.astype(jnp.float32)
    slot_id = lax.broadcasted_iota(jnp.int32, (half, rows), 0).astype(jnp.float32)
    pick_low = jnp.where(mine & (slot_row == slot_id), 1.0, 0.0).astype(jnp.bfloat16)
    pick_high = jnp.where(mine & (slot_row == slot_id + half), 1.0, 0.0).astype(jnp.bfloat16)

    def multiply(c):
        gate_copy(c).wait()
        up_copy(c).wait()
        where = pl.ds(pl.multiple_of(c * depth, depth), depth)
        piece = left[c]
        gate_acc[...] += jnp.dot(piece, gate_in[where], preferred_element_type=jnp.float32)
        up_acc[...] += jnp.dot(piece, up_in[where], preferred_element_type=jnp.float32)

    shrink_copy.wait()

    @pl.loop(0, pieces + 2)
    def _(s):
        @pl.when(s < pieces)
        def _():
            each(line - 1, lambda d: z_copy(s, d).wait_recv())
            if pairs > 1:
                y_copy(s).start()

        @pl.when((s >= 1) & (s < pieces + 1))
        def _():
            c = s - 1
            if pairs > 1:
                y_copy(c).wait_recv()
            c_copy(c).start()

        @pl.when(s >= 2)
        def _():
            c = s - 2
            c_copy(c).wait_recv()
            blocks = [
                rows_in[c, kk, yy, zz].astype(jnp.float32)
                for zz in range(line) for yy in range(pairs) for kk in range(CORES)
            ]
            piece = jnp.concatenate(blocks, axis=0).astype(jnp.bfloat16)
            left[c] = piece
            where = pl.ds(pl.multiple_of(c * depth, depth), depth)
            shrink_acc[...] += jnp.dot(piece, shrink_in[where], preferred_element_type=jnp.float32)

        @pl.when(s >= 2 + LAG)
        def _():
            multiply(s - 2 - LAG)

    shrunk = shrink_acc[...]
    shrunk = jnp.concatenate([shrunk, shrunk], axis=1).astype(jnp.bfloat16)
    lane_p = lax.broadcasted_iota(jnp.int32, (half, 2 * rank), 1)
    low = jnp.dot(pick_low, shrunk, preferred_element_type=jnp.float32)
    high = jnp.dot(pick_high, shrunk, preferred_element_type=jnp.float32)
    packed[me] = jnp.where(lane_p < rank, low, high).astype(jnp.bfloat16)
    each(total - 1, lambda i: p_copy(i).start())

    @pl.loop(pieces - LAG, pieces)
    def _(c):
        multiply(c)

    for c in range(pieces):
        each(line - 1, lambda d, c=c: z_copy(c, d).wait_send())
        if pairs > 1:
            y_copy(c).wait_send()
        c_copy(c).wait_send()
    wait_all(id_rows, id_send)

    expand_copy.wait()
    wait_all(packed, p_recv)
    wait_all(packed, p_send)
    id_col = slots_of[0][:, :1]
    slot_col = slots_of[1][:, :1]
    in_high = slot_col >= half
    at = id_col * half + jnp.where(in_high, slot_col - half, slot_col)
    column = lax.broadcasted_iota(jnp.int32, (rows, total * half), 1).astype(jnp.float32)
    pick = jnp.where(column == at, 1.0, 0.0).astype(jnp.bfloat16)
    found = jnp.dot(
        pick, packed[...].reshape(total * half, 2 * rank), preferred_element_type=jnp.float32
    )
    turned = jnp.concatenate([found[:, rank:], found[:, :rank]], axis=1)
    lane_r = lax.broadcasted_iota(jnp.int32, (rows, 2 * rank), 1)
    both = jnp.where((lane_r < rank) != in_high, found, turned)
    second = jnp.where(lane_r < rank, 0.0, 1.0)
    for j in range(adapters // 2):
        wide[:, j * 2 * rank:(j + 1) * 2 * rank] = jnp.where(
            id_col == second + 2.0 * j, both, 0.0).astype(jnp.bfloat16)
    delta = jnp.dot(wide[...], expand_in[...], preferred_element_type=jnp.float32)
    out[...] = (jax.nn.silu(gate_acc[...]) * (up_acc[...] + delta)).astype(jnp.bfloat16)


def local(pairs, tokens, adapter_ids, gate_weight, up_weight, shrink_factors, expand_factors):
    total = lax.axis_size("tensor")
    line = total // (pairs * CORES)
    row_dev, width = tokens.shape
    rows = row_dev * total
    hidden = gate_weight.shape[1]
    adapters, rank, _ = expand_factors.shape
    half = 2 * row_dev
    pieces = 8
    depth = width // pieces
    anywhere = pl.BlockSpec(memory_space=pl.ANY)
    dma = pltpu.SemaphoreType.DMA
    bf16, f32 = jnp.bfloat16, jnp.float32
    return pl.pallas_call(
        functools.partial(step_kernel, line, pairs, pieces),
        out_shape=jax.ShapeDtypeStruct((rows, hidden), bf16),
        in_specs=[anywhere, pl.BlockSpec(memory_space=pltpu.SMEM)] + [anywhere] * 4,
        out_specs=pl.BlockSpec(memory_space=pltpu.VMEM),
        scratch_shapes=[
            pltpu.VMEM((pieces, CORES, pairs, line, row_dev, depth), bf16),
            pltpu.VMEM((width, hidden), bf16),
            pltpu.VMEM((width, hidden), bf16),
            pltpu.VMEM((width, rank), bf16),
            pltpu.VMEM((adapters * rank, hidden), bf16),
            pltpu.VMEM((pieces, rows, depth), bf16),
            pltpu.VMEM((rows, hidden), f32),
            pltpu.VMEM((rows, hidden), f32),
            pltpu.VMEM((rows, rank), f32),
            pltpu.VMEM((total, 1, rows), jnp.int32),
            pltpu.VMEM((total, half, 2 * rank), bf16),
            pltpu.VMEM((2, rows, 128), f32),
            pltpu.VMEM((rows, adapters * rank), bf16),
            dma((pieces,)), dma((pieces,)), dma((pieces,)), dma((2,)),
            dma((pieces, line - 1)), dma((pieces, line - 1)),
            dma((pieces,)), dma((pieces,)), dma((pieces,)), dma((pieces,)),
            dma, dma, dma, dma,
        ],
        compiler_params=pltpu.CompilerParams(
            collective_id=0, has_side_effects=True, vmem_limit_bytes=58 * 2**20
        ),
        cost_estimate=pl.CostEstimate(
            flops=4 * rows * width * hidden,
            bytes_accessed=4 * width * hidden,
            transcendentals=rows * hidden,
        ),
    )(
        tokens, adapter_ids, gate_weight, up_weight,
        shrink_factors.reshape(width, rank), expand_factors.reshape(adapters * rank, hidden),
    )


def solution(mesh):
    pairs = 2 if mesh.shape["tensor"] == 16 else 1
    return jax.shard_map(
        functools.partial(local, pairs),
        mesh=mesh,
        in_specs=(
            P(("groups", "tensor"), None),
            P(("groups", "tensor")),
            P(None, "tensor"),
            P(None, "tensor"),
            P("tensor", None, None),
            P(None, None, "tensor"),
        ),
        out_specs=P("groups", "tensor"),
        check_vma=False,
    )
```

time: 142 us -> 49.9 us (0.35)
  blocking collectives: 73.2 us -> 0 us
  Pallas kernels: 0 us -> 45.2 us
  waiting for transfers between devices: 27.7 us -> 0 us
  between operations: 14.1 us -> 0.01 us
  matrix products: 13.8 us -> 0 us
  local copies, waits for them, and re-layouts: 9.32 us -> 4.45 us
  other arithmetic: 3.31 us -> 0 us
    psum x1 -> x0, blocking collectives: 59.5 us -> none  [local(): shrunk = lax.psum(partial_sum, 'tensor').astype(jnp.bfloat16)]
    pallas_call x0 -> x1, Pallas kernels: none -> 45.2 us  [local(): pl.pallas_call(functools.partial(step_kernel, line, pairs, pieces), out_s...]
    all_gather x1 -> x0, waiting for transfers between devices: 27 us -> none  [local(): lax.all_gather(tokens, 'tensor', axis=0, tiled=True)]
    dot_general x4 -> x0, matrix products: 13.8 us -> none  [the longest x1 8.41 us: absorb_rows(): jnp.dot(piece_rows, gate_weight, preferred_element_type=jnp.float32)]
    unnamed x1 -> x0, blocking collectives: 13.7 us -> none
    gather x2 -> x0, local copies, waits for them, and re-layouts: 3.91 us -> none  [the longest x1 3.2 us: local(): chosen_rows = jnp.take(rows_all, chosen, axis=0)]
    sort x1 -> x0, other arithmetic: 2.54 us -> none  [local(): chosen = jnp.argsort(order_keys)[:capacity]]
    unnamed x9 -> x2, local copies, waits for them, and re-layouts: 5.35 us -> 4.45 us
  transfers between devices with their start and end apart: 1 -> 0, of which waited for: 1 -> 0; matrix products, arithmetic and copies ran while one was open for 4% -> 0% of each run, Pallas kernels for 0% -> 0%
where the time goes in v1:
time: 49.9 us; the launch traced here: 49.7 us
  Pallas kernels  45.2 us (91%)
  local copies, waits for them, and re-layouts  4.45 us (9%)
    pallas_call x1, Pallas kernels, local(): pl.pallas_call(functools.partial(step_kernel, line, pairs, pieces), out_s...  45.2 us
    unnamed x2, local copies, waits for them, and re-layouts  4.45 us

profile of v1, /device:TPU:0, one launch (start us, length us, event | category | flops | bytes accessed | tf_op | source)
XLA Modules:
  0.0 49.7 jit_solution(709537503224344123)
XLA Ops:
  0.0 2.8 %copy.7 = bf16[1,8192,64]{2,1,0:T(8,128)(2,1)} copy(bf16[1,8192,64]{1,2,0:T(8,128)(2,1)} %param.10) | data formatting | bytes 2097152 | tf_op args[4]
  2.8 45.2 %shard_map.64 = bf16[128,1024]{1,0:T(8,128)(2,1)} custom-call(bf16[8,8192]{1,0:T(8,128)(2,1)} %tokens.1, s32[8]{0:T(128)} %ids.1, bf16[8192,1024]{1,0:T(8,128)(2,1)} %gate_weight.1, bf16[8192,1024]{1,0:T(8,128)(2,1)} %up_weight.1, bf16[8192,64]{1,0:T(8,128)(2,1)} %bitcast.2, bf16[1024,1024]{1,0:T(8,128)(2,1)} %bitcast.3), custom_call_target="tpu_custom_call" | custom-call | flops 4294967296 | bytes 33554432 | tf_op jit(solution)/shard_map/pallas_call | solution.py:247
  48.0 1.7 %copy.9 = bf16[128,1024]{1,0:T(8,128)(2,1)} copy(bf16[128,1024]{1,0:T(8,128)(2,1)} %shard_map.64) | data formatting | bytes 524288

commit v2 on v1

--- a/solution.py
+++ b/solution.py
@@ -8,7 +8,11 @@
 from jax.sharding import PartitionSpec as P
 
 CORES = 2
-LAG = 2
+SKEW = 2
+LAG = 6
+EARLY = 2
+ID_STEP = 3
+AHEAD = 3
 
 
 def each(count, body):
@@ -24,7 +28,7 @@
     tokens, ids, gate_weight, up_weight, shrink, expand,
     out,
     rows_in, gate_in, up_in, shrink_in, expand_in, left, gate_acc, up_acc, shrink_acc,
-    id_rows, packed, slots_of, wide,
+    id_rows, packed, slots_of, picks, wide,
     own_sem, gate_sem, up_sem, small_sem, z_send, z_recv, y_send, y_recv, c_send, c_recv,
     id_send, id_recv, p_send, p_recv,
 ):
@@ -32,7 +36,7 @@
     row_dev = tokens.shape[0]
     rows = total * row_dev
     depth = tokens.shape[1] // pieces
-    rank = shrink.shape[1]
+    rank = shrink.shape[0]
     half = packed.shape[1]
     adapters = expand.shape[0] // rank
 
@@ -107,10 +111,9 @@
     for c in range(pieces):
         own_copy(c).start()
     shrink_copy.start()
-    for c in range(pieces):
+    for c in range(EARLY):
         gate_copy(c).start()
         up_copy(c).start()
-    expand_copy.start()
 
     lane = lax.broadcasted_iota(jnp.int32, (1, rows), 1)
     id_row = jnp.zeros((1, rows), jnp.int32)
@@ -124,28 +127,29 @@
         own_copy(c).wait()
 
     pl.semaphore_wait(barrier, total - 1)
-    for c in range(pieces):
+    for c in range(AHEAD):
         each(line - 1, lambda d, c=c: z_copy(c, d).start())
         if c == 0:
             each(total - 1, lambda i: id_copy(i).start())
 
-    wait_all(id_rows, id_recv)
-    owner = lax.broadcasted_iota(jnp.int32, (total, 1, rows), 0)
-    lane3 = lax.broadcasted_iota(jnp.int32, (total, 1, rows), 2)
-    id_row = jnp.sum(jnp.where(lane3 // row_dev == owner, id_rows[...], 0), axis=0)
-    across = lax.broadcasted_iota(jnp.int32, (rows, rows), 1)
-    down = lax.broadcasted_iota(jnp.int32, (rows, rows), 0)
-    id_wide = jnp.broadcast_to(id_row, (rows, rows)).astype(jnp.float32)
-    id_col = jnp.sum(jnp.where(across == down, id_wide, 0.0), axis=1, keepdims=True)
-    same = jnp.where(id_wide == id_col, 1.0, 0.0)
-    slot_col = jnp.sum(jnp.where(across < down, same, 0.0), axis=1, keepdims=True)
-    slot_row = jnp.sum(jnp.where(down < across, same, 0.0), axis=0, keepdims=True)
-    slots_of[0] = jnp.broadcast_to(id_col, (rows, 128))
-    slots_of[1] = jnp.broadcast_to(slot_col, (rows, 128))
-    mine = id_row.astype(jnp.float32) == me.astype(jnp.float32)
-    slot_id = lax.broadcasted_iota(jnp.int32, (half, rows), 0).astype(jnp.float32)
-    pick_low = jnp.where(mine & (slot_row == slot_id), 1.0, 0.0).astype(jnp.bfloat16)
-    pick_high = jnp.where(mine & (slot_row == slot_id + half), 1.0, 0.0).astype(jnp.bfloat16)
+    def place_rows():
+        wait_all(id_rows, id_recv)
+        owner = lax.broadcasted_iota(jnp.int32, (total, 1, rows), 0)
+        lane3 = lax.broadcasted_iota(jnp.int32, (total, 1, rows), 2)
+        id_row = jnp.sum(jnp.where(lane3 // row_dev == owner, id_rows[...], 0), axis=0)
+        across = lax.broadcasted_iota(jnp.int32, (rows, rows), 1)
+        down = lax.broadcasted_iota(jnp.int32, (rows, rows), 0)
+        id_wide = jnp.broadcast_to(id_row, (rows, rows)).astype(jnp.float32)
+        id_col = jnp.sum(jnp.where(across == down, id_wide, 0.0), axis=1, keepdims=True)
+        same = jnp.where(id_wide == id_col, 1.0, 0.0)
+        slot_col = jnp.sum(jnp.where(across < down, same, 0.0), axis=1, keepdims=True)
+        slot_row = jnp.sum(jnp.where(down < across, same, 0.0), axis=0, keepdims=True)
+        slots_of[0] = jnp.broadcast_to(id_col, (rows, 128))
+        slots_of[1] = jnp.broadcast_to(slot_col, (rows, 128))
+        mine = id_row.astype(jnp.float32) == me.astype(jnp.float32)
+        slot_id = lax.broadcasted_iota(jnp.int32, (half, rows), 0).astype(jnp.float32)
+        picks[0] = jnp.where(mine & (slot_row == slot_id), 1.0, 0.0).astype(jnp.bfloat16)
+        picks[1] = jnp.where(mine & (slot_row == slot_id + half), 1.0, 0.0).astype(jnp.bfloat16)
 
     def multiply(c):
         gate_copy(c).wait()
@@ -157,7 +161,7 @@
 
     shrink_copy.wait()
 
-    @pl.loop(0, pieces + 2)
+    @pl.loop(0, pieces + 2 * SKEW)
     def _(s):
         @pl.when(s < pieces)
         def _():
@@ -165,16 +169,33 @@
             if pairs > 1:
                 y_copy(s).start()
 
-        @pl.when((s >= 1) & (s < pieces + 1))
-        def _():
-            c = s - 1
+        @pl.when(s + AHEAD < pieces)
+        def _():
+            each(line - 1, lambda d: z_copy(s + AHEAD, d).start())
+
+        @pl.when(s + EARLY < pieces)
+        def _():
+            gate_copy(s + EARLY).start()
+            up_copy(s + EARLY).start()
+
+        @pl.when(s == pieces - EARLY)
+        def _():
+            expand_copy.start()
+
+        @pl.when((s >= SKEW) & (s < pieces + SKEW))
+        def _():
+            c = s - SKEW
             if pairs > 1:
                 y_copy(c).wait_recv()
             c_copy(c).start()
 
-        @pl.when(s >= 2)
-        def _():
-            c = s - 2
+        @pl.when(s == ID_STEP)
+        def _():
+            place_rows()
+
+        @pl.when(s >= 2 * SKEW)
+        def _():
+            c = s - 2 * SKEW
             c_copy(c).wait_recv()
             blocks = [
                 rows_in[c, kk, yy, zz].astype(jnp.float32)
@@ -183,17 +204,20 @@
             piece = jnp.concatenate(blocks, axis=0).astype(jnp.bfloat16)
             left[c] = piece
             where = pl.ds(pl.multiple_of(c * depth, depth), depth)
-            shrink_acc[...] += jnp.dot(piece, shrink_in[where], preferred_element_type=jnp.float32)
-
-        @pl.when(s >= 2 + LAG)
-        def _():
-            multiply(s - 2 - LAG)
+            shrink_acc[...] += lax.dot_general(
+                piece, shrink_in[:, where], (((1,), (1,)), ((), ())),
+                preferred_element_type=jnp.float32,
+            )
+
+        @pl.when(s >= 2 * SKEW + LAG)
+        def _():
+            multiply(s - 2 * SKEW - LAG)
 
     shrunk = shrink_acc[...]
     shrunk = jnp.concatenate([shrunk, shrunk], axis=1).astype(jnp.bfloat16)
     lane_p = lax.broadcasted_iota(jnp.int32, (half, 2 * rank), 1)
-    low = jnp.dot(pick_low, shrunk, preferred_element_type=jnp.float32)
-    high = jnp.dot(pick_high, shrunk, preferred_element_type=jnp.float32)
+    low = jnp.dot(picks[0], shrunk, preferred_element_type=jnp.float32)
+    high = jnp.dot(picks[1], shrunk, preferred_element_type=jnp.float32)
     packed[me] = jnp.where(lane_p < rank, low, high).astype(jnp.bfloat16)
     each(total - 1, lambda i: p_copy(i).start())
 
@@ -253,7 +277,7 @@
             pltpu.VMEM((pieces, CORES, pairs, line, row_dev, depth), bf16),
             pltpu.VMEM((width, hidden), bf16),
             pltpu.VMEM((width, hidden), bf16),
-            pltpu.VMEM((width, rank), bf16),
+            pltpu.VMEM((rank, width), bf16),
             pltpu.VMEM((adapters * rank, hidden), bf16),
             pltpu.VMEM((pieces, rows, depth), bf16),
             pltpu.VMEM((rows, hidden), f32),
@@ -262,6 +286,7 @@
             pltpu.VMEM((total, 1, rows), jnp.int32),
             pltpu.VMEM((total, half, 2 * rank), bf16),
             pltpu.VMEM((2, rows, 128), f32),
+            pltpu.VMEM((2, half, rows), bf16),
             pltpu.VMEM((rows, adapters * rank), bf16),
             dma((pieces,)), dma((pieces,)), dma((pieces,)), dma((2,)),
             dma((pieces, line - 1)), dma((pieces, line - 1)),
@@ -278,7 +303,7 @@
         ),
     )(
         tokens, adapter_ids, gate_weight, up_weight,
-        shrink_factors.reshape(width, rank), expand_factors.reshape(adapters * rank, hidden),
+        shrink_factors[0].T, expand_factors.reshape(adapters * rank, hidden),
     )
 
 

time: 49.9 us -> 35.6 us (0.71)
  Pallas kernels: 45.2 us -> 33.7 us
  local copies, waits for them, and re-layouts: 4.45 us -> 1.67 us
    pallas_call x1, Pallas kernels: 45.2 us -> 33.7 us  [local(): pl.pallas_call(functools.partial(step_kernel, line, pairs, pieces), out_s...]
    unnamed x2 -> x1, local copies, waits for them, and re-layouts: 4.45 us -> 1.67 us
where the time goes in v2:
time: 35.6 us; the launch traced here: 35.4 us
  Pallas kernels  33.7 us (95%)
  local copies, waits for them, and re-layouts  1.67 us (5%)
    pallas_call x1, Pallas kernels, local(): pl.pallas_call(functools.partial(step_kernel, line, pairs, pieces), out_s...  33.7 us
    unnamed x1, local copies, waits for them, and re-layouts  1.67 us

profile of v2, /device:TPU:0, one launch (start us, length us, event | category | flops | bytes accessed | tf_op | source)
XLA Modules:
  0.0 35.4 jit_solution(9183790698957024087)
XLA Ops:
  0.0 33.7 %shard_map.64 = bf16[128,1024]{1,0:T(8,128)(2,1)} custom-call(bf16[8,8192]{1,0:T(8,128)(2,1)} %tokens.1, s32[8]{0:T(128)} %ids.1, bf16[8192,1024]{1,0:T(8,128)(2,1)} %gate_weight.1, bf16[8192,1024]{1,0:T(8,128)(2,1)} %up_weight.1, bf16[64,8192]{1,0:T(8,128)(2,1)} %bitcast.5, bf16[1024,1024]{1,0:T(8,128)(2,1)} %bitcast.4), custom_call_target="tpu_custom_call" | custom-call | flops 4294967296 | bytes 33554432 | tf_op jit(solution)/shard_map/pallas_call | solution.py:271
  33.7 1.7 %copy.8 = bf16[128,1024]{1,0:T(8,128)(2,1)} copy(bf16[128,1024]{1,0:T(8,128)(2,1)} %shard_map.64) | data formatting | bytes 524288

commit v3 on v2

--- a/solution.py
+++ b/solution.py
@@ -8,10 +8,10 @@
 from jax.sharding import PartitionSpec as P
 
 CORES = 2
-SKEW = 2
-LAG = 6
-EARLY = 2
-ID_STEP = 3
+SKEW = 1
+LAG = 4
+EARLY = 1
+ID_STEP = 4
 AHEAD = 3
 
 
@@ -53,7 +53,7 @@
 
     def own_copy(c):
         return pltpu.make_async_copy(
-            tokens.at[:, pl.ds(c * depth, depth)], rows_in.at[c, k, y, z], own_sem.at[c]
+            tokens.at[:, pl.ds(c * depth, depth)], rows_in.at[c, k, y, 0], own_sem.at[c]
         )
 
     def gate_copy(c):
@@ -68,16 +68,22 @@
     expand_copy = pltpu.make_async_copy(expand, expand_in, small_sem.at[1])
 
     def z_copy(c, d):
-        block = rows_in.at[c, k, y, z]
-        return pltpu.make_async_remote_copy(
-            block, block, z_send.at[c, d], z_recv.at[c, d],
+        return pltpu.make_async_remote_copy(
+            rows_in.at[c, k, y, 0], rows_in.at[c, k, y, line - 1 - d], z_send.at[c, d], z_recv.at[c, d],
             device_id=place(lax.rem(z + d + 1, line), y, k), device_id_type=pl.DeviceIdType.MESH,
         )
 
+    def y_own(c):
+        block = rows_in.at[c, k, y, 0]
+        return pltpu.make_async_remote_copy(
+            block, block, y_send.at[0, c], y_recv.at[0, c],
+            device_id=place(z, 1 - y, k), device_id_type=pl.DeviceIdType.MESH,
+        )
+
     def y_copy(c):
-        block = rows_in.at[c, k, y]
-        return pltpu.make_async_remote_copy(
-            block, block, y_send.at[c], y_recv.at[c],
+        block = rows_in.at[c, k, y, pl.ds(1, line - 1)]
+        return pltpu.make_async_remote_copy(
+            block, block, y_send.at[1, c], y_recv.at[1, c],
             device_id=place(z, 1 - y, k), device_id_type=pl.DeviceIdType.MESH,
         )
 
@@ -129,8 +135,10 @@
     pl.semaphore_wait(barrier, total - 1)
     for c in range(AHEAD):
         each(line - 1, lambda d, c=c: z_copy(c, d).start())
-        if c == 0:
-            each(total - 1, lambda i: id_copy(i).start())
+    if pairs > 1:
+        for c in range(pieces):
+            y_own(c).start()
+    each(total - 1, lambda i: id_copy(i).start())
 
     def place_rows():
         wait_all(id_rows, id_recv)
@@ -186,6 +194,7 @@
         def _():
             c = s - SKEW
             if pairs > 1:
+                y_own(c).wait_recv()
                 y_copy(c).wait_recv()
             c_copy(c).start()
 
@@ -198,7 +207,7 @@
             c = s - 2 * SKEW
             c_copy(c).wait_recv()
             blocks = [
-                rows_in[c, kk, yy, zz].astype(jnp.float32)
+                rows_in[c, kk, yy, lax.rem(zz - z + line, line)].astype(jnp.float32)
                 for zz in range(line) for yy in range(pairs) for kk in range(CORES)
             ]
             piece = jnp.concatenate(blocks, axis=0).astype(jnp.bfloat16)
@@ -228,6 +237,7 @@
     for c in range(pieces):
         each(line - 1, lambda d, c=c: z_copy(c, d).wait_send())
         if pairs > 1:
+            y_own(c).wait_send()
             y_copy(c).wait_send()
         c_copy(c).wait_send()
     wait_all(id_rows, id_send)
@@ -263,7 +273,7 @@
     hidden = gate_weight.shape[1]
     adapters, rank, _ = expand_factors.shape
     half = 2 * row_dev
-    pieces = 8
+    pieces = 4
     depth = width // pieces
     anywhere = pl.BlockSpec(memory_space=pl.ANY)
     dma = pltpu.SemaphoreType.DMA
@@ -290,7 +300,7 @@
             pltpu.VMEM((rows, adapters * rank), bf16),
             dma((pieces,)), dma((pieces,)), dma((pieces,)), dma((2,)),
             dma((pieces, line - 1)), dma((pieces, line - 1)),
-            dma((pieces,)), dma((pieces,)), dma((pieces,)), dma((pieces,)),
+            dma((2, pieces)), dma((2, pieces)), dma((pieces,)), dma((pieces,)),
             dma, dma, dma, dma,
         ],
         compiler_params=pltpu.CompilerParams(

time: 35.6 us -> 34.3 us (0.963)
  the two profiles are of different devices: /device:TPU:0 before, /device:TPU:11 now
where the time goes in v3:
time: 34.3 us; the launch traced here: 34.2 us
  Pallas kernels  32.5 us (95%)
  local copies, waits for them, and re-layouts  1.67 us (5%)
    pallas_call x1, Pallas kernels, local(): pl.pallas_call(functools.partial(step_kernel, line, pairs, pieces), out_s...  32.5 us
    unnamed x1, local copies, waits for them, and re-layouts  1.67 us

profile of v3, /device:TPU:11, one launch (start us, length us, event | category | flops | bytes accessed | tf_op | source)
XLA Modules:
  0.0 34.2 jit_solution(6850724187663471260)
XLA Ops:
  0.0 32.5 %shard_map.64 = bf16[128,1024]{1,0:T(8,128)(2,1)} custom-call(bf16[8,8192]{1,0:T(8,128)(2,1)} %tokens.1, s32[8]{0:T(128)} %ids.1, bf16[8192,1024]{1,0:T(8,128)(2,1)} %gate_weight.1, bf16[8192,1024]{1,0:T(8,128)(2,1)} %up_weight.1, bf16[64,8192]{1,0:T(8,128)(2,1)} %bitcast.5, bf16[1024,1024]{1,0:T(8,128)(2,1)} %bitcast.4), custom_call_target="tpu_custom_call" | custom-call | flops 4294967296 | bytes 33554432 | tf_op jit(solution)/shard_map/pallas_call | solution.py:281
  32.5 1.7 %copy.8 = bf16[128,1024]{1,0:T(8,128)(2,1)} copy(bf16[128,1024]{1,0:T(8,128)(2,1)} %shard_map.64) | data formatting | bytes 524288
